TPU v7x, 256 devices: a whole 4x4x8 slice. The times are simulated.
256 devices in a mesh: dp: 16 (over z, core), expert: 4 (over y), blk: 4 (over x).
Axes of the slice: x: 4, y: 4, z: 8, core: 2. Of those that a mesh axis runs over, the one named last changes fastest.
Arguments:
- tokens: bfloat16 [2048, 6144], P('dp', 'blk'), may hold values from -6 to 6
- expert_ids: int32 [2048, 2], P('dp'), may hold values from 0 to 7, all different within a row; in each aligned block of 128 rows (0 to 127, 128 to 255, ...) at most 48 rows name the same one
- route_weights: float32 [2048, 2], P('dp'), may hold values from 0.1 to 1
- gate_weight: bfloat16 [8, 6144, 8192], P('expert', 'blk', 'dp'), may hold values from -0.078125 to 0.078125
- up_weight: bfloat16 [8, 6144, 8192], P('expert', 'blk', 'dp'), may hold values from -0.078125 to 0.078125
- down_weight: bfloat16 [8, 8192, 6144], P('expert', 'dp', 'blk'), may hold values from -0.0625 to 0.0625
Outputs:
- mixed: bfloat16 [2048, 6144], P('dp', 'blk')
Inputs may be any that keep to these rules, and one draw needn't show every extreme that they name: `expert_ids`: each row names 2 different experts. Among the 128 rows of one data shard no expert is named more than 48 times, and in every draw some expert is named exactly 48 times in some shard.
All inputs are finite; a program needn't handle non-finite values.
Results may differ from a plain program's by a relative error of at most 0.0051.
Values may be sent and summed in bfloat16 or wider, within the bound.
A program may use at most 64 MiB of HBM per device.

v0:
```python
import jax
import jax.numpy as jnp
from jax import lax
from jax.sharding import PartitionSpec as P

EXPERTS = 8
CAP = 48


def local(tokens, expert_ids, route_weights, gate_weight, up_weight, down_weight):
    local_count = gate_weight.shape[0]
    token_count = tokens.shape[0]
    top_count = expert_ids.shape[1]
    group_index = lax.axis_index("expert")
    flat_ids = expert_ids.reshape(-1)
    one_hot = (flat_ids[:, None] == jnp.arange(EXPERTS, dtype=jnp.int32)[None, :]).astype(jnp.int32)
    before = jnp.cumsum(one_hot, axis=0) - one_hot
    position = jnp.sum(before * one_hot, axis=1)
    local_ids = flat_ids - group_index * local_count
    is_mine = local_ids[:, None] == jnp.arange(local_count, dtype=jnp.int32)[None, :]
    in_slot = position[:, None] == jnp.arange(CAP, dtype=jnp.int32)[None, :]
    slot_hit = (is_mine[:, :, None] & in_slot[:, None, :]).reshape(
        token_count, top_count, local_count, CAP
    )
    dispatch = jnp.any(slot_hit, axis=1).astype(jnp.bfloat16)
    combine = jnp.sum(slot_hit.astype(jnp.float32) * route_weights[:, :, None, None], axis=1)
    picked = jnp.einsum("tec,tf->ecf", dispatch, tokens, preferred_element_type=jnp.float32).astype(
        jnp.bfloat16
    )
    shard_rows = lax.all_gather(picked, "dp", axis=1, tiled=True)
    gate_part = jnp.einsum(
        "enf,efh->enh", shard_rows, gate_weight, preferred_element_type=jnp.float32
    )
    up_part = jnp.einsum("enf,efh->enh", shard_rows, up_weight, preferred_element_type=jnp.float32)
    partial_value = jnp.stack([gate_part, up_part])
    summed = lax.psum(partial_value, "blk")
    hidden = (jax.nn.silu(summed[0]) * summed[1]).astype(jnp.bfloat16)
    expert_out = lax.psum_scatter(
        jnp.einsum("enh,ehd->ned", hidden, down_weight, preferred_element_type=jnp.float32),
        "dp",
        scatter_dimension=0,
        tiled=True,
    )
    mixed_part = jnp.einsum("tec,ced->td", combine, expert_out, precision=lax.Precision.HIGHEST)
    mixed = lax.psum(mixed_part, "expert")
    return mixed.astype(jnp.bfloat16)


def solution(mesh):
    placed = (
        P("dp", "blk"),
        P("dp", None),
        P("dp", None),
        P("expert", "blk", "dp"),
        P("expert", "blk", "dp"),
        P("expert", "dp", "blk"),
    )
    return jax.shard_map(
        local, mesh=mesh, in_specs=placed, out_specs=P("dp", "blk"), check_vma=False
    )
```

profile of v0, /device:TPU:2, one launch (start us, length us, event | category | flops | bytes accessed | tf_op | source)
XLA Modules:
  0.0 316.2 jit_solution(18314517861227424447)
XLA Ops:
  6.5 0.0 copy-start
  6.5 0.0 all-gather.2.cloned.1.call-start
  6.5 0.9 copy.13
  7.5 0.1 eq.65
  7.6 0.1 reshape.70
  7.8 0.6 reduce-window.6
  8.4 0.2 slice_reduce_fusion
  8.6 0.1 fusion.7
  8.7 0.1 eq.69
  8.9 0.1 copy.15
  9.0 0.7 broadcast_subtract_fusion
  9.7 1.9 convolution_convert_fusion
  11.6 0.0 all-gather.2.cloned.1.call-update
  11.7 0.0 all-reduce.3.cloned.1.call-start
  11.7 45.8 %all-gather.2.cloned.1.call-done = bf16[2,768,1536]{2,1,0:T(8,128)(2,1)} async-done(((bf16[2,48,1536]{2,1,0:T(8,128)(2,1)}), bf16[2,768,1536]{2,1,0:T(8,128)(2,1)}) %all-gather.2.cloned.1.call-update) | async-done | bytes 4718608 | tf_op jit(solution)/shard_map/all_gather | solution.py:30
  57.5 0.0 copy-start.2
  57.5 0.0 copy-start.3
  57.5 5.5 %convolution_bitcast_fusion.2 = f32[1,2,768,512]{3,2,1,0:T(8,128)S(1)} fusion(bf16[2,768,1536]{2,1,0:T(8,128)(2,1)} %all-gather.2.cloned.1.call-done, bf16[2,1536,512]{2,1,0:T(8,128)(2,1)} %param.10), kind=kOutput, calls=%fused_computation.8 | convolution fusion | flops 2415919104 | bytes 11010048 | tf_op jit(solution)/shard_map/enf,efh->enh/dot_general | solution.py:34
  63.0 0.0 copy-done.2
  63.0 0.1 copy-done.3
  63.1 2.6 convolution_bitcast_fusion.3
  65.7 3.4 %pad_maximum_fusion = f32[2,2,768,512]{3,2,1,0:T(8,128)} fusion(f32[1,2,768,512]{3,2,1,0:T(8,128)S(1)} %convolution_bitcast_fusion.2, f32[1,2,768,512]{3,2,1,0:T(8,128)S(1)} %convolution_bitcast_fusion.3), kind=kLoop, calls=%fused_computation | loop fusion | flops 1572864 | bytes 12582912 | tf_op jit(solution)/shard_map/stack | solution.py:35
  69.1 0.0 all-reduce.3.cloned.1.call-update
  69.1 0.0 reduce-scatter.2.cloned.1.call-start
  69.1 129.7 %all-reduce.3.cloned.1.call-done = f32[2,2,768,512]{3,2,1,0:T(8,128)} async-done(((f32[2,2,768,512]{3,2,1,0:T(8,128)}), f32[2,2,768,512]{3,2,1,0:T(8,128)}) %all-reduce.3.cloned.1.call-update) | async-done | bytes 6291472 | tf_op jit(solution)/shard_map/psum | solution.py:36
  198.9 0.0 copy-done
  198.9 8.0 %convolution_bitcast_fusion = f32[768,2,1536]{2,0,1:T(8,128)} fusion(bf16[2,512,1536]{2,1,0:T(8,128)(2,1)S(1)} %copy-done, f32[2,2,768,512]{3,2,1,0:T(8,128)} %all-reduce.3.cloned.1.call-done), kind=kOutput, calls=%fused_computation.1 | convolution fusion | flops 2420637696 | bytes 18874368 | tf_op jit(solution)/shard_map/enh,ehd->ned/dot_general | solution.py:39
  206.9 0.0 copy-start.1
  206.9 0.0 reduce-scatter.2.cloned.1.call-update
  206.9 0.7 copy-done.1
  207.6 73.1 %reduce-scatter.2.cloned.1.call-done = f32[48,2,1536]{2,0,1:T(8,128)} async-done(((f32[768,2,1536]{2,0,1:T(8,128)}), f32[48,2,1536]{2,0,1:T(8,128)}) %reduce-scatter.2.cloned.1.call-update) | async-done | bytes 589840 | tf_op jit(solution)/shard_map/reduce_scatter | solution.py:38
  280.7 2.8 convolution_bitcast_fusion.1
  283.5 26.3 %all-reduce.4 = bf16[128,1536]{1,0:T(8,128)(2,1)} all-reduce(f32[128,1536]{1,0:T(8,128)} %convolution_bitcast_fusion.1), channel_id=1, replica_groups=mesh['dp'=16,'expert'=4,'blk'=4] {'expert'}, use_global_device_ids=true, to_apply=%region_7.8 | all-reduce | flops 196608 | bytes 1179648 | tf_op jit(solution)/shard_map/psum | solution.py:45
  (7 shorter events, 0.1 us)
Async XLA Ops:
  6.5 192.3 %copy-start = (bf16[2,512,1536]{2,1,0:T(8,128)(2,1)S(1)}, bf16[2,512,1536]{2,1,0:T(8,128)(2,1)}, u32[]{:S(2)}) copy-start(bf16[2,512,1536]{2,1,0:T(8,128)(2,1)} %param.11) | copy-start | bytes 9437188
  6.5 50.9 %all-gather.2.cloned.1.call-start = ((), (), s32[]{:S(2)}) async-start(), calls=%async_computation.1 | async-start | bytes 5013504 | tf_op jit(solution)/shard_map/all_gather | solution.py:30
  11.7 187.2 %all-reduce.3.cloned.1.call-start = ((), (), s32[]{:S(2)}) async-start(), calls=%async_computation.2 | async-start | bytes 12582912 | tf_op jit(solution)/shard_map/psum | solution.py:36
  57.5 5.6 %copy-start.2 = (bf16[2,768,1536]{2,1,0:T(8,128)(2,1)S(1)}, bf16[2,768,1536]{2,1,0:T(8,128)(2,1)}, u32[]{:S(2)}) copy-start(bf16[2,768,1536]{2,1,0:T(8,128)(2,1)} %all-gather.2.cloned.1.call-done) | copy-start | bytes 14155780
  57.5 5.6 %copy-start.3 = (bf16[2,1536,512]{2,1,0:T(8,128)(2,1)S(1)}, bf16[2,1536,512]{2,1,0:T(8,128)(2,1)}, u32[]{:S(2)}) copy-start(bf16[2,1536,512]{2,1,0:T(8,128)(2,1)} %param.9) | copy-start | bytes 9437188
  69.1 211.6 %reduce-scatter.2.cloned.1.call-start = ((), (), s32[]{:S(2)}) async-start(), calls=%async_computation.3 | async-start | bytes 10027008 | tf_op jit(solution)/shard_map/reduce_scatter | solution.py:38
  206.9 0.7 copy-start.1
Sparse Core Ops, SparseCore 0:
  11.8 45.6 all-gather.1
  69.2 129.6 all-reduce.2
  207.0 73.5 reduce-scatter.1
where the time goes:
time: 316 us
  waiting for transfers between devices  249 us (79%)
  blocking collectives  26.3 us (8%)
  matrix products  20.9 us (7%)
  between operations  13.2 us (4%)
  other arithmetic  4.85 us (2%)
    psum x1, waiting for transfers between devices, local(): summed = lax.psum(partial_value, 'blk')  130 us
    reduce_scatter x1, waiting for transfers between devices, local(): lax.psum_scatter(jnp.einsum('enh,ehd->ned', hidden, down_weight, preferre...  73.1 us
    all_gather x1, waiting for transfers between devices, local(): shard_rows = lax.all_gather(picked, 'dp', axis=1, tiled=True)  45.8 us
    psum x1, blocking collectives, local(): mixed = lax.psum(mixed_part, 'expert')  26.3 us
    dot_general x1, matrix products, local(): jnp.einsum('enh,ehd->ned', hidden, down_weight, preferred_element_type=jn...  8.03 us
  transfers between devices with their start and end apart: 3, of which 3 were waited for; matrix products, arithmetic and copies ran while one was open for 0% of the time, Pallas kernels for 0%

commit v1 on v0

--- a/solution.py
+++ b/solution.py
@@ -42,7 +42,7 @@
         tiled=True,
     )
     mixed_part = jnp.einsum("tec,ced->td", combine, expert_out, precision=lax.Precision.HIGHEST)
-    mixed = lax.psum(mixed_part, "expert")
+    mixed = jnp.sum(lax.all_gather(mixed_part, "expert"), axis=0)
     return mixed.astype(jnp.bfloat16)
 
 

time: 316 us -> 336 us (1.063)
  waiting for transfers between devices: 249 us -> 290 us
  blocking collectives: 26.3 us -> 0 us
    all_gather x0 -> x1, waiting for transfers between devices: none -> 41.6 us  [local(): mixed = jnp.sum(lax.all_gather(mixed_part, 'expert'), axis=0)]
    psum x1 -> x0, blocking collectives: 26.3 us -> none  [local(): mixed = lax.psum(mixed_part, 'expert')]
  transfers between devices with their start and end apart: 3 -> 4, of which waited for: 3 -> 4; matrix products, arithmetic and copies ran while one was open for 0% -> 0% of each run, Pallas kernels for 0% -> 0%
where the time goes in v1:
time: 336 us; the launch traced here: 335 us
  waiting for transfers between devices  290 us (86%)
  matrix products  20.9 us (6%)
  between operations  13.2 us (4%)
  other arithmetic  7.83 us (2%)
    psum x1, waiting for transfers between devices, local(): summed = lax.psum(partial_value, 'blk')  130 us
    reduce_scatter x1, waiting for transfers between devices, local(): lax.psum_scatter(jnp.einsum('enh,ehd->ned', hidden, down_weight, preferre...  73.2 us
    all_gather x1, waiting for transfers between devices, local(): shard_rows = lax.all_gather(picked, 'dp', axis=1, tiled=True)  45.8 us
    all_gather x1, waiting for transfers between devices, local(): mixed = jnp.sum(lax.all_gather(mixed_part, 'expert'), axis=0)  41.6 us
    dot_general x1, matrix products, local(): jnp.einsum('enh,ehd->ned', hidden, down_weight, preferred_element_type=jn...  8.04 us
  transfers between devices with their start and end apart: 4, of which 4 were waited for; matrix products, arithmetic and copies ran while one was open for 0% of the time, Pallas kernels for 0%

profile of v1, /device:TPU:2, one launch (start us, length us, event | category | flops | bytes accessed | tf_op | source)
XLA Modules:
  0.0 334.7 jit_solution(3512961565734179631)
XLA Ops:
  6.5 0.0 copy-start
  6.5 0.0 all-gather.4.cloned.1.call-start
  6.5 0.9 copy.13
  7.5 0.1 eq.65
  7.6 0.1 reshape.70
  7.8 0.6 reduce-window.6
  8.4 0.2 slice_reduce_fusion
  8.6 0.1 fusion.7
  8.7 0.1 eq.69
  8.9 0.1 copy.15
  9.0 0.7 broadcast_subtract_fusion
  9.7 1.9 convolution_convert_fusion
  11.6 0.0 all-gather.4.cloned.1.call-update
  11.6 0.0 all-reduce.2.cloned.1.call-start
  11.7 45.8 %all-gather.4.cloned.1.call-done = bf16[2,768,1536]{2,1,0:T(8,128)(2,1)} async-done(((bf16[2,48,1536]{2,1,0:T(8,128)(2,1)}), bf16[2,768,1536]{2,1,0:T(8,128)(2,1)}) %all-gather.4.cloned.1.call-update) | async-done | bytes 4718608 | tf_op jit(solution)/shard_map/all_gather | solution.py:30
  57.5 0.0 copy-start.2
  57.5 0.0 copy-start.3
  57.5 5.5 %convolution_bitcast_fusion.2 = f32[1,2,768,512]{3,2,1,0:T(8,128)S(1)} fusion(bf16[2,768,1536]{2,1,0:T(8,128)(2,1)} %all-gather.4.cloned.1.call-done, bf16[2,1536,512]{2,1,0:T(8,128)(2,1)} %param.10), kind=kOutput, calls=%fused_computation.8 | convolution fusion | flops 2415919104 | bytes 11010048 | tf_op jit(solution)/shard_map/enf,efh->enh/dot_general | solution.py:34
  63.0 0.0 copy-done.2
  63.0 0.1 copy-done.3
  63.1 2.6 convolution_bitcast_fusion.3
  65.7 3.4 %pad_maximum_fusion = f32[2,2,768,512]{3,2,1,0:T(8,128)} fusion(f32[1,2,768,512]{3,2,1,0:T(8,128)S(1)} %convolution_bitcast_fusion.2, f32[1,2,768,512]{3,2,1,0:T(8,128)S(1)} %convolution_bitcast_fusion.3), kind=kLoop, calls=%fused_computation | loop fusion | flops 1572864 | bytes 12582912 | tf_op jit(solution)/shard_map/stack | solution.py:35
  69.1 0.0 all-reduce.2.cloned.1.call-update
  69.1 0.0 reduce-scatter.2.cloned.1.call-start
  69.1 129.7 %all-reduce.2.cloned.1.call-done = f32[2,2,768,512]{3,2,1,0:T(8,128)} async-done(((f32[2,2,768,512]{3,2,1,0:T(8,128)}), f32[2,2,768,512]{3,2,1,0:T(8,128)}) %all-reduce.2.cloned.1.call-update) | async-done | bytes 6291472 | tf_op jit(solution)/shard_map/psum | solution.py:36
  198.9 0.0 copy-done
  198.9 8.0 %convolution_bitcast_fusion = f32[768,2,1536]{2,0,1:T(8,128)} fusion(bf16[2,512,1536]{2,1,0:T(8,128)(2,1)S(1)} %copy-done, f32[2,2,768,512]{3,2,1,0:T(8,128)} %all-reduce.2.cloned.1.call-done), kind=kOutput, calls=%fused_computation.1 | convolution fusion | flops 2420637696 | bytes 18874368 | tf_op jit(solution)/shard_map/enh,ehd->ned/dot_general | solution.py:39
  206.9 0.0 copy-start.1
  206.9 0.0 reduce-scatter.2.cloned.1.call-update
  206.9 0.0 all-gather.6.cloned.1.call-start
  207.0 0.6 copy-done.1
  207.6 73.2 %reduce-scatter.2.cloned.1.call-done = f32[48,2,1536]{2,0,1:T(8,128)} async-done(((f32[768,2,1536]{2,0,1:T(8,128)}), f32[48,2,1536]{2,0,1:T(8,128)}) %reduce-scatter.2.cloned.1.call-update) | async-done | bytes 589840 | tf_op jit(solution)/shard_map/reduce_scatter | solution.py:38
  280.8 2.8 convolution_bitcast_fusion.1
  283.6 0.0 all-gather.6.cloned.1.call-update
  283.6 41.6 %all-gather.6.cloned.1.call-done = f32[512,1536]{1,0:T(8,128)} async-done(((f32[128,1536]{1,0:T(8,128)}), f32[512,1536]{1,0:T(8,128)}) %all-gather.6.cloned.1.call-update) | async-done | bytes 3145744 | tf_op jit(solution)/shard_map/all_gather | solution.py:45
  325.2 3.0 reduce_sum.29
  (7 shorter events, 0.1 us)
Async XLA Ops:
  6.5 192.3 %copy-start = (bf16[2,512,1536]{2,1,0:T(8,128)(2,1)S(1)}, bf16[2,512,1536]{2,1,0:T(8,128)(2,1)}, u32[]{:S(2)}) copy-start(bf16[2,512,1536]{2,1,0:T(8,128)(2,1)} %param.11) | copy-start | bytes 9437188
  6.5 50.9 %all-gather.4.cloned.1.call-start = ((), (), s32[]{:S(2)}) async-start(), calls=%async_computation.1 | async-start | bytes 5013504 | tf_op jit(solution)/shard_map/all_gather | solution.py:30
  11.6 187.2 %all-reduce.2.cloned.1.call-start = ((), (), s32[]{:S(2)}) async-start(), calls=%async_computation.2 | async-start | bytes 12582912 | tf_op jit(solution)/shard_map/psum | solution.py:36
  57.5 5.6 %copy-start.2 = (bf16[2,768,1536]{2,1,0:T(8,128)(2,1)S(1)}, bf16[2,768,1536]{2,1,0:T(8,128)(2,1)}, u32[]{:S(2)}) copy-start(bf16[2,768,1536]{2,1,0:T(8,128)(2,1)} %all-gather.4.cloned.1.call-done) | copy-start | bytes 14155780
  57.5 5.6 %copy-start.3 = (bf16[2,1536,512]{2,1,0:T(8,128)(2,1)S(1)}, bf16[2,1536,512]{2,1,0:T(8,128)(2,1)}, u32[]{:S(2)}) copy-start(bf16[2,1536,512]{2,1,0:T(8,128)(2,1)} %param.9) | copy-start | bytes 9437188
  69.1 211.7 %reduce-scatter.2.cloned.1.call-start = ((), (), s32[]{:S(2)}) async-start(), calls=%async_computation.3 | async-start | bytes 10027008 | tf_op jit(solution)/shard_map/reduce_scatter | solution.py:38
  206.9 0.7 copy-start.1
  206.9 118.2 %all-gather.6.cloned.1.call-start = ((), (), s32[]{:S(2)}) async-start(), calls=%async_computation.4 | async-start | bytes 3932160 | tf_op jit(solution)/shard_map/all_gather | solution.py:45
Sparse Core Ops, SparseCore 0:
  11.8 45.6 all-gather.3
  69.2 129.6 all-reduce.1
  207.1 73.7 reduce-scatter.1
  283.7 41.3 all-gather.5

commit v2 on v0

--- a/solution.py
+++ b/solution.py
@@ -27,7 +27,9 @@
     picked = jnp.einsum("tec,tf->ecf", dispatch, tokens, preferred_element_type=jnp.float32).astype(
         jnp.bfloat16
     )
-    shard_rows = lax.all_gather(picked, "dp", axis=1, tiled=True)
+    shard_rows = jnp.concatenate(
+        lax.all_to_all(jnp.stack([picked] * lax.axis_size("dp")), "dp", 0, 0), axis=1
+    )
     gate_part = jnp.einsum(
         "enf,efh->enh", shard_rows, gate_weight, preferred_element_type=jnp.float32
     )

time: 316 us -> 384 us (1.22)
  blocking collectives: 26.3 us -> 141 us
  waiting for transfers between devices: 249 us -> 203 us
    all_to_all x0 -> x1, blocking collectives: none -> 114 us  [local(): lax.all_to_all(jnp.stack([picked] * lax.axis_size('dp')), 'dp', 0, 0)]
    all_gather x1 -> x0, waiting for transfers between devices: 45.8 us -> none  [local(): shard_rows = lax.all_gather(picked, 'dp', axis=1, tiled=True)]
  transfers between devices with their start and end apart: 3 -> 2, of which waited for: 3 -> 2; matrix products, arithmetic and copies ran while one was open for 0% -> 0% of each run, Pallas kernels for 0% -> 0%
where the time goes in v2:
time: 384 us
  waiting for transfers between devices  203 us (53%)
  blocking collectives  141 us (37%)
  matrix products  17.2 us (4%)
  between operations  13.5 us (4%)
  other arithmetic  4.9 us (1%)
  local copies, waits for them, and re-layouts  4.7 us (1%)
    psum x1, waiting for transfers between devices, local(): summed = lax.psum(partial_value, 'blk')  130 us
    all_to_all x1, blocking collectives, local(): lax.all_to_all(jnp.stack([picked] * lax.axis_size('dp')), 'dp', 0, 0)  114 us
    reduce_scatter x1, waiting for transfers between devices, local(): lax.psum_scatter(jnp.einsum('enh,ehd->ned', hidden, down_weight, preferre...  73 us
    psum x1, blocking collectives, local(): mixed = lax.psum(mixed_part, 'expert')  26.4 us
    dot_general x1, matrix products, local(): jnp.einsum('enh,ehd->ned', hidden, down_weight, preferred_element_type=jn...  8.04 us
  transfers between devices with their start and end apart: 2, of which 2 were waited for; matrix products, arithmetic and copies ran while one was open for 0% of the time, Pallas kernels for 0%

profile of v2, /device:TPU:2, one launch (start us, length us, event | category | flops | bytes accessed | tf_op | source)
XLA Modules:
  0.0 383.7 jit_solution(17837398546231954809)
XLA Ops:
  6.5 0.0 copy-start
  6.5 0.0 all-reduce.3.cloned.1.call-start
  6.5 0.9 copy.18
  7.5 0.1 eq.65
  7.6 0.1 reshape.78
  7.8 0.6 reduce-window.6
  8.4 0.2 slice_reduce_fusion
  8.6 0.1 fusion.7
  8.7 0.1 eq.69
  8.9 0.1 copy.20
  9.0 0.7 broadcast_subtract_fusion
  9.7 1.2 convolution_convert_fusion
  10.9 0.5 stack.8
  11.4 114.3 %all_to_all.5 = bf16[16,2,48,1536]{3,2,1,0:T(8,128)(2,1)S(1)} all-to-all(bf16[16,2,48,1536]{3,2,1,0:T(8,128)(2,1)S(1)} %stack.8), channel_id=1, replica_groups=mesh['dp'=16,'expert'=4,'blk'=4] {'dp'}, dimensions={0} | all-to-all | bytes 9437184 | tf_op jit(solution)/shard_map/all_to_all | solution.py:31
  125.7 0.0 copy-start.2
  125.7 0.4 copy.21
  126.1 1.5 copy-done.2
  127.6 0.0 copy-start.3
  127.6 2.6 convolution_bitcast_fusion.2
  130.2 0.0 copy-done.3
  130.2 2.6 convolution_bitcast_fusion.3
  132.8 3.4 pad_maximum_fusion
  136.2 0.0 all-reduce.3.cloned.1.call-update
  136.3 0.0 reduce-scatter.2.cloned.1.call-start
  136.3 129.6 %all-reduce.3.cloned.1.call-done = f32[2,2,768,512]{3,2,1,0:T(8,128)} async-done(((f32[2,2,768,512]{3,2,1,0:T(8,128)}), f32[2,2,768,512]{3,2,1,0:T(8,128)}) %all-reduce.3.cloned.1.call-update) | async-done | bytes 6291472 | tf_op jit(solution)/shard_map/psum | solution.py:38
  266.0 0.0 copy-done
  266.0 8.0 %convolution_bitcast_fusion = f32[768,2,1536]{2,0,1:T(8,128)} fusion(bf16[2,512,1536]{2,1,0:T(8,128)(2,1)S(1)} %copy-done, f32[2,2,768,512]{3,2,1,0:T(8,128)} %all-reduce.3.cloned.1.call-done), kind=kOutput, calls=%fused_computation.1 | convolution fusion | flops 2420637696 | bytes 18874368 | tf_op jit(solution)/shard_map/enh,ehd->ned/dot_general | solution.py:41
  274.0 0.0 copy-start.1
  274.0 0.0 reduce-scatter.2.cloned.1.call-update
  274.0 0.7 copy-done.1
  274.7 73.0 %reduce-scatter.2.cloned.1.call-done = f32[48,2,1536]{2,0,1:T(8,128)} async-done(((f32[768,2,1536]{2,0,1:T(8,128)}), f32[48,2,1536]{2,0,1:T(8,128)}) %reduce-scatter.2.cloned.1.call-update) | async-done | bytes 589840 | tf_op jit(solution)/shard_map/reduce_scatter | solution.py:40
  347.7 2.8 convolution_bitcast_fusion.1
  350.4 26.4 %all-reduce.4 = bf16[128,1536]{1,0:T(8,128)(2,1)} all-reduce(f32[128,1536]{1,0:T(8,128)} %convolution_bitcast_fusion.1), channel_id=1, replica_groups=mesh['dp'=16,'expert'=4,'blk'=4] {'expert'}, use_global_device_ids=true, to_apply=%region_7.8 | all-reduce | flops 196608 | bytes 1179648 | tf_op jit(solution)/shard_map/psum | solution.py:47
  (7 shorter events, 0.1 us)
Async XLA Ops:
  6.5 259.4 %copy-start = (bf16[2,512,1536]{2,1,0:T(8,128)(2,1)S(1)}, bf16[2,512,1536]{2,1,0:T(8,128)(2,1)}, u32[]{:S(2)}) copy-start(bf16[2,512,1536]{2,1,0:T(8,128)(2,1)} %param.11) | copy-start | bytes 9437188
  6.5 259.4 %all-reduce.3.cloned.1.call-start = ((), (), s32[]{:S(2)}) async-start(), calls=%async_computation.2 | async-start | bytes 12582912 | tf_op jit(solution)/shard_map/psum | solution.py:38
  125.7 1.9 copy-start.2
  127.6 2.6 copy-start.3
  136.3 211.4 %reduce-scatter.2.cloned.1.call-start = ((), (), s32[]{:S(2)}) async-start(), calls=%async_computation.3 | async-start | bytes 10027008 | tf_op jit(solution)/shard_map/reduce_scatter | solution.py:40
  274.0 0.7 copy-start.1
Sparse Core Ops, SparseCore 0:
  136.4 129.5 all-reduce.2
  274.1 73.4 reduce-scatter.1
